TPU v7x, 32 devices: a whole 2x2x4 slice. The times are simulated.
32 devices in a mesh: grid: 8 (over z, y), sub: 4 (over x, core).
Axes of the slice: x: 2, y: 2, z: 4, core: 2. Of those that a mesh axis runs over, the one named last changes fastest.
Arguments:
- field: float32 [5, 256, 32, 128], P(None, ('grid', 'sub')), may hold values from -6 to 6
- node_jitter: float32 [3, 256, 32, 128], P(None, ('grid', 'sub')), may hold values from -0.15 to 0.15
- time_ratio: float32 [256, 32, 128], P(('grid', 'sub')), may hold values from 0.2 to 5
- donor_cell: int32 [32, 8, 2, 128], P(('grid', 'sub')), may hold values from 0 to 32638, as said below
- receptor_offset: float32 [32, 8, 2, 3, 128], P(('grid', 'sub')), may hold values from 0.1 to 0.9
- receptor_node: int32 [32, 8, 2, 128], P(('grid', 'sub')), may hold values from 4096 to 28671, as said below
- point_count: int32 [32, 8], P(('grid', 'sub')), may hold values from 1 to 256, as said below
Outputs:
- relaxed: float32 [5, 256, 32, 128], P(None, ('grid', 'sub'))
Inputs may be any that keep to these rules, and one draw needn't show every extreme that they name: `donor_cell`: a cell i * 32 * 128 + j * 128 + k with i < 8, j < 31, k < 127. `receptor_node`: distinct over all slots of one source block, on local planes 1 to 6. `point_count`: from every block of grid g, owner (g + 1) mod 8 receives exactly 256 points, owner (g + 2) mod 8 receives one point, and every other owner at most 128.
All inputs are finite; a program needn't handle non-finite values.
Results may differ from a plain program's by a relative error of at most 0.0003.
Values sent between devices are 32-bit elements; how exact they have to be, the bound alone decides.
No kernel may reach another device: no remote copies, remote signals or barrier semaphores. Data moves between devices by JAX's collectives and lax.ppermute only.
A program may use at most 128 MiB of HBM per device.

v0:
```python
import jax
import jax.numpy as jnp
from jax import lax
from jax.sharding import PartitionSpec as P


def passed_along(value, axis, steps):
    count = lax.axis_size(axis)
    pairs = [(source, (source + steps) % count) for source in range(count)]
    return lax.ppermute(value, axis, pairs)


def extended_2(cells, sides, width):
    for axis, dim in sides:
        count = lax.axis_size(axis)
        head = lax.slice_in_dim(cells, 0, width, axis=dim)
        tail = lax.slice_in_dim(cells, cells.shape[dim] - width, cells.shape[dim], axis=dim)
        cells = jnp.concatenate(
            [
                lax.ppermute(tail, axis, [(i, (i + 1) % count) for i in range(count)]),
                cells,
                lax.ppermute(head, axis, [((i + 1) % count, i) for i in range(count)]),
            ],
            axis=dim,
        )
    return cells


def corner_bits(corner):
    return (corner >> 2 & 1, corner >> 1 & 1, corner & 1)


def shape_values(param):
    result = []
    for corner in range(8):
        offset_bits = corner_bits(corner)
        factors = [
            param[axis_id] if offset_bits[axis_id] else 1.0 - param[axis_id] for axis_id in range(3)
        ]
        derivs = [1.0 if offset_bits[axis_id] else -1.0 for axis_id in range(3)]
        weight = factors[0] * factors[1] * factors[2]
        slopes = [
            derivs[0] * factors[1] * factors[2],
            factors[0] * derivs[1] * factors[2],
            factors[0] * factors[1] * derivs[2],
        ]
        result.append((weight, slopes))
    return result


def determinant(matrix):
    return (
        matrix[0][0] * (matrix[1][1] * matrix[2][2] - matrix[1][2] * matrix[2][1])
        - matrix[0][1] * (matrix[1][0] * matrix[2][2] - matrix[1][2] * matrix[2][0])
        + matrix[0][2] * (matrix[1][0] * matrix[2][1] - matrix[1][1] * matrix[2][0])
    )


def solve_point(corners, offsets):
    target = [offsets[..., component, :] for component in range(3)]
    places = [
        [
            corners[corner, component] + float(corner_bits(corner)[component])
            for component in range(3)
        ]
        for corner in range(8)
    ]
    param = [jnp.full(target[0].shape, 0.5, target[0].dtype) for component in range(3)]
    for newton_step in range(4):
        shapes = shape_values(param)
        misfit = []
        jacobian = []
        for component in range(3):
            position = shapes[0][0] * places[0][component]
            for corner in range(1, 8):
                position = position + shapes[corner][0] * places[corner][component]
            misfit.append(position - target[component])
            jac_row = []
            for direction in range(3):
                slope_sum = shapes[0][1][direction] * places[0][component]
                for corner in range(1, 8):
                    slope_sum = slope_sum + shapes[corner][1][direction] * places[corner][component]
                jac_row.append(slope_sum)
            jacobian.append(jac_row)
        jac_det = determinant(jacobian)
        updates = []
        for direction in range(3):
            replaced = [
                [
                    misfit[component] if column == direction else jacobian[component][column]
                    for column in range(3)
                ]
                for component in range(3)
            ]
            updates.append(determinant(replaced) / jac_det)
        param = [param[direction] - updates[direction] for direction in range(3)]
    shapes = shape_values(param)
    values = []
    for variable in range(corners.shape[1] - 3):
        blended = shapes[0][0] * corners[0, 3 + variable]
        for corner in range(1, 8):
            blended = blended + shapes[corner][0] * corners[corner, 3 + variable]
        values.append(blended)
    return jnp.stack(values, axis=-2)


def gather_corners(data_flat, cells, plane_size, row_size):
    picks = []
    for corner in range(8):
        offset_bits = corner_bits(corner)
        shift_amount = offset_bits[0] * plane_size + offset_bits[1] * row_size + offset_bits[2]
        picks.append(data_flat[:, cells + shift_amount])
    return jnp.stack(picks, 0)


def fill_fringe(own, values, nodes, counts):
    width = own.shape[0]
    interp = jnp.moveaxis(values, 2, 0).reshape(width, -1)
    slot_count, point_total = (nodes.shape[1], nodes.shape[2])
    position = (
        jnp.arange(slot_count, dtype=jnp.int32)[:, None] * point_total
        + jnp.arange(point_total, dtype=jnp.int32)[None, :]
    )
    live = (position[None] < counts[:, None, None]).reshape(-1)
    flat_nodes = nodes.reshape(-1)
    current = own[:, flat_nodes]
    own = own.at[:, flat_nodes].set(jnp.where(live[None], interp, current))
    flags = jnp.zeros((own.shape[1],), own.dtype).at[flat_nodes].set(live.astype(own.dtype))
    return (own, flags)


def neighbour_sum(above, below, filled):
    lead = [(0, 0)] * (filled.ndim - 2)
    padded_y = jnp.pad(filled, lead + [(1, 1), (0, 0)])
    padded_z = jnp.pad(filled, lead + [(0, 0), (1, 1)])
    return (
        above
        + below
        + padded_y[..., 2:, :]
        + padded_y[..., :-2, :]
        + padded_z[..., 2:]
        + padded_z[..., :-2]
    )


def relax(filled, above, below, ratio, flags):
    smooth = (filled + ratio * neighbour_sum(above, below, filled)) / (1.0 + 6.0 * ratio)
    return jnp.where(flags > 0.5, filled, smooth)


def on_device(
    field, node_jitter, time_ratio, donor_cell, receptor_offset, receptor_node, point_count
):
    width, planes, rows_count, cols_count = field.shape
    stacked = jnp.concatenate([node_jitter, field], 0)
    following = passed_along(stacked[:, :1], "sub", -1)
    extended = jnp.concatenate([stacked, following], 1)
    ext_flat = extended.reshape(extended.shape[0], -1)
    plane_size = rows_count * cols_count
    cells = lax.all_to_all(donor_cell, "grid", split_axis=1, concat_axis=1, tiled=True)
    offsets = lax.all_to_all(receptor_offset, "grid", split_axis=1, concat_axis=1, tiled=True)
    corners = gather_corners(ext_flat, cells, plane_size, cols_count)
    values_here = solve_point(corners, offsets)
    values = lax.all_to_all(values_here, "grid", split_axis=1, concat_axis=1, tiled=True)
    own = field.reshape(width, -1)
    filled, flags = fill_fringe(own, values[0], receptor_node[0], point_count[0])
    filled = filled.reshape(width, planes, rows_count, cols_count)
    flags = flags.reshape(planes, rows_count, cols_count)
    padded = extended_2(filled, (("sub", 1),), 1)
    above = padded[:, 2:]
    below = padded[:, :-2]
    return relax(filled, above, below, time_ratio, flags)


def solution(mesh):
    placed = (
        P(None, ("grid", "sub"), None, None),
        P(None, ("grid", "sub"), None, None),
        P(("grid", "sub"), None, None),
        P(("grid", "sub"), None, None, None),
        P(("grid", "sub"), None, None, None, None),
        P(("grid", "sub"), None, None, None),
        P(("grid", "sub"), None),
    )
    return jax.shard_map(
        on_device,
        mesh=mesh,
        in_specs=placed,
        out_specs=P(None, ("grid", "sub"), None, None),
        check_vma=False,
    )
```

profile of v0, /device:TPU:0, one launch (start us, length us, event | category | flops | bytes accessed | tf_op | source)
XLA Modules:
  0.0 198.9 jit_solution(1316684340209411117)
XLA Ops:
  0.0 7.3 %all-to-all-start = ((s32[1,8,2,128]{3,2,0,1:T(2,128)}), s32[1,8,2,128]{3,2,0,1:T(2,128)S(1)}, u32[]{:S(2)}, u32[]{:S(2)}) async-start(s32[1,8,2,128]{3,2,0,1:T(2,128)} %bitcast.2284), calls=%async_computation | async-start | bytes 16384 | tf_op jit(solution)/shard_map/all_to_all | solution.py:160
  7.3 1.0 constant_dynamic-update-slice_fusion.1
  8.3 1.1 constant_dynamic-update-slice_fusion
  9.5 0.7 collective-permute-start
  10.2 0.7 compare_select_fusion
  10.9 0.1 iota_add_fusion
  11.0 0.7 broadcast_compare_fusion.1
  11.7 8.1 %scatter_custom_fusion = f32[32768]{0:T(1024)S(1)} fusion(s32[2048]{0:T(1024)S(1)} %bitcast.2279, f32[2048]{0:T(1024)S(1)} %convert_element_type.7, f32[]{:T(128)} %constant.8.clone.1), kind=kCustom, calls=%fused_computation.33 | custom fusion | bytes 131076 | tf_op jit(solution)/shard_map/scatter | solution.py:128
  19.8 0.0 all-to-all-done
  19.8 5.7 %all-to-all-start.1 = ((f32[1,8,2,3,128]{4,2,3,0,1:T(2,128)}), f32[1,8,2,3,128]{4,2,3,0,1:T(2,128)S(1)}, u32[]{:S(2)}, u32[]{:S(2)}) async-start(f32[1,8,2,3,128]{4,2,3,0,1:T(2,128)} %bitcast.2282), calls=%async_computation.1 | async-start | bytes 49152 | tf_op jit(solution)/shard_map/all_to_all | solution.py:161
  25.7 6.5 %all-to-all-done.1 = f32[1,8,2,3,128]{4,2,3,0,1:T(2,128)S(1)} async-done(((f32[1,8,2,3,128]{4,2,3,0,1:T(2,128)}), f32[1,8,2,3,128]{4,2,3,0,1:T(2,128)S(1)}, u32[]{:S(2)}, u32[]{:S(2)}) %all-to-all-start.1) | async-done | bytes 24608 | tf_op jit(solution)/shard_map/all_to_all | solution.py:161
  32.2 0.0 collective-permute-done
  32.2 0.1 pad_maximum_fusion
  32.4 0.0 copy-start
  32.4 9.8 %copy.203 = f32[8,9,32,128]{0,3,2,1:T(8,128)} copy(f32[8,9,32,128]{3,2,1,0:T(8,128)S(1)} %pad_maximum_fusion) | data formatting | bytes 2359296 | tf_op jit(solution)/shard_map/concatenate | solution.py:157
  42.1 11.8 %gather_fusion.1 = f32[2048,8]{1,0:T(8,128)S(1)} fusion(f32[8,36864]{0,1:T(8,128)} %bitcast.2124, s32[2048]{0:T(1024)S(1)} %get-tuple-element.127), kind=kCustom, calls=%fused_computation.1 | custom fusion | bytes 139264 | tf_op jit(solution)/shard_map/gather | solution.py:112
  54.0 0.3 copy.208
  54.3 11.9 %gather_fusion.2 = f32[2048,8]{1,0:T(8,128)S(1)} fusion(f32[8,36864]{0,1:T(8,128)} %bitcast.2125, s32[2048]{0:T(1024)S(1)} %get-tuple-element.126), kind=kCustom, calls=%fused_computation.2 | custom fusion | bytes 139264 | tf_op jit(solution)/shard_map/gather | solution.py:112
  66.1 0.3 copy.210
  66.4 11.9 %gather_fusion.3 = f32[2048,8]{1,0:T(8,128)S(1)} fusion(f32[8,36864]{0,1:T(8,128)} %bitcast.2126, s32[2048]{0:T(1024)S(1)} %get-tuple-element.125), kind=kCustom, calls=%fused_computation.3 | custom fusion | bytes 139264 | tf_op jit(solution)/shard_map/gather | solution.py:112
  78.3 0.3 copy.212
  78.6 11.9 %gather_fusion.4 = f32[2048,8]{1,0:T(8,128)S(1)} fusion(f32[8,36864]{0,1:T(8,128)} %bitcast.2127, s32[2048]{0:T(1024)S(1)} %get-tuple-element.124), kind=kCustom, calls=%fused_computation.4 | custom fusion | bytes 139264 | tf_op jit(solution)/shard_map/gather | solution.py:112
  90.4 0.3 copy.214
  90.7 11.9 %gather_fusion.5 = f32[2048,8]{1,0:T(8,128)S(1)} fusion(f32[8,36864]{0,1:T(8,128)} %bitcast.2128, s32[2048]{0:T(1024)S(1)} %get-tuple-element.123), kind=kCustom, calls=%fused_computation.5 | custom fusion | bytes 139264 | tf_op jit(solution)/shard_map/gather | solution.py:112
  102.6 0.3 copy.216
  102.9 11.9 %gather_fusion.6 = f32[2048,8]{1,0:T(8,128)S(1)} fusion(f32[8,36864]{0,1:T(8,128)} %bitcast.2129, s32[2048]{0:T(1024)S(1)} %get-tuple-element.122), kind=kCustom, calls=%fused_computation.6 | custom fusion | bytes 139264 | tf_op jit(solution)/shard_map/gather | solution.py:112
  114.7 0.3 copy.218
  115.0 11.9 %gather_fusion.7 = f32[2048,8]{1,0:T(8,128)S(1)} fusion(f32[8,36864]{0,1:T(8,128)} %bitcast.2130, s32[2048]{0:T(1024)S(1)} %get-tuple-element.121), kind=kCustom, calls=%fused_computation.7 | custom fusion | bytes 139264 | tf_op jit(solution)/shard_map/gather | solution.py:112
  126.9 0.3 copy.220
  127.2 11.9 %gather_fusion = f32[2048,8]{1,0:T(8,128)S(1)} fusion(f32[8,36864]{0,1:T(8,128)} %bitcast.2131, s32[2048]{0:T(1024)S(1)} %broadcast_clamp_fusion.8), kind=kCustom, calls=%fused_computation | custom fusion | bytes 139264 | tf_op jit(solution)/shard_map/gather | solution.py:112
  139.0 0.3 copy.206
  139.3 0.1 multiply_subtract_fusion.18
  139.4 0.1 multiply_subtract_fusion.13
  139.6 0.1 multiply_add_fusion.21
  139.6 0.1 multiply_subtract_fusion.8
  139.7 0.1 multiply_add_fusion.11
  139.8 0.1 multiply_subtract_fusion.2
  139.9 0.1 divide_subtract_fusion.1
  140.1 0.6 copy.253
  140.8 3.3 %all-to-all-start.2 = ((f32[1,8,2,5,128]{4,2,3,0,1:T(2,128)}), f32[1,8,2,5,128]{4,2,3,0,1:T(2,128)S(1)}, u32[]{:S(2)}, u32[]{:S(2)}) async-start(f32[1,8,2,5,128]{4,2,3,0,1:T(2,128)} %copy.253), calls=%async_computation.2 | async-start | bytes 81920 | tf_op jit(solution)/shard_map/all_to_all | solution.py:164
  144.1 0.0 copy-done
  144.2 8.8 %copy.202 = f32[5,8,32,128]{0,3,2,1:T(8,128)} copy(f32[5,8,32,128]{3,2,1,0:T(8,128)S(1)} %copy-done) | data formatting | bytes 1310720 | tf_op args[0]
  152.9 0.0 all-to-all-done.2
  152.9 0.4 copy.254
  153.3 29.7 %scatter_custom_fusion.1 = f32[5,32768]{0,1:T(8,128)} fusion(f32[5,32768]{0,1:T(8,128)} %bitcast.2122, s32[2048]{0:T(1024)S(1)} %bitcast.2281, f32[5,2048]{0,1:T(8,128)S(1)} %bitcast.2132, pred[2048]{0:T(1024)(128)(4,1)S(1)} %lt.64, s32[2048]{0:T(1024)S(1)} %get-tuple-element.120), kind=kCustom, calls=%fused_computation.14 | custom fusion | flops 10240 | bytes 2369536 | tf_op jit(solution)/shard_map/scatter | solution.py:127
  183.0 0.0 copy-start.1
  183.0 10.1 %copy.262 = f32[5,8,32,128]{3,2,1,0:T(8,128)S(1)} copy(f32[5,8,32,128]{0,3,2,1:T(8,128)} %bitcast.2123) | data formatting | bytes 1310720 | tf_op jit(solution)/shard_map/reshape | solution.py:167
  193.1 0.1 collective-permute-start.1
  193.2 0.5 collective-permute-start.2
  193.7 0.0 copy-done.1
  193.7 1.7 collective-permute-done.1
  195.4 2.2 %collective-permute-done.2 = f32[5,1,32,128]{3,2,1,0:T(8,128)S(1)} collective-permute-done((f32[5,1,32,128]{3,2,1,0:T(8,128)S(1)}, f32[5,1,32,128]{3,2,1,0:T(8,128)S(1)}, u32[]{:S(2)}, u32[]{:S(2)}) %collective-permute-start.2) | collective-permute-done | bytes 81952 | tf_op jit(solution)/shard_map/ppermute | solution.py:20
  197.6 1.2 fusion.9
  (24 shorter events, 0.4 us)
Async XLA Ops:
  0.0 19.8 %all-to-all-start = ((s32[1,8,2,128]{3,2,0,1:T(2,128)}), s32[1,8,2,128]{3,2,0,1:T(2,128)S(1)}, u32[]{:S(2)}, u32[]{:S(2)}) async-start(s32[1,8,2,128]{3,2,0,1:T(2,128)} %bitcast.2284), calls=%async_computation | async-start | bytes 16384 | tf_op jit(solution)/shard_map/all_to_all | solution.py:160
  9.5 22.7 %collective-permute-start = (f32[8,1,32,128]{3,2,1,0:T(8,128)S(1)}, f32[8,1,32,128]{3,2,1,0:T(8,128)S(1)}, u32[]{:S(2)}, u32[]{:S(2)}) collective-permute-start(f32[8,1,32,128]{3,2,1,0:T(8,128)S(1)} %slice.324), channel_id=1, source_target_pairs={{0,3},{1,0},{2,1},{3,2},{4,7},{5,4},{6,5},{7,6},{8,11},{9,8},{10,9... | collective-permute-start | bytes 393224 | tf_op jit(solution)/shard_map/ppermute | solution.py:10
  19.8 12.4 %all-to-all-start.1 = ((f32[1,8,2,3,128]{4,2,3,0,1:T(2,128)}), f32[1,8,2,3,128]{4,2,3,0,1:T(2,128)S(1)}, u32[]{:S(2)}, u32[]{:S(2)}) async-start(f32[1,8,2,3,128]{4,2,3,0,1:T(2,128)} %bitcast.2282), calls=%async_computation.1 | async-start | bytes 49152 | tf_op jit(solution)/shard_map/all_to_all | solution.py:161
  32.4 111.8 %copy-start = (f32[5,8,32,128]{3,2,1,0:T(8,128)S(1)}, f32[5,8,32,128]{3,2,1,0:T(8,128)}, u32[]{:S(2)}) copy-start(f32[5,8,32,128]{3,2,1,0:T(8,128)} %param.7) | copy-start | bytes 1966084
  140.8 12.1 %all-to-all-start.2 = ((f32[1,8,2,5,128]{4,2,3,0,1:T(2,128)}), f32[1,8,2,5,128]{4,2,3,0,1:T(2,128)S(1)}, u32[]{:S(2)}, u32[]{:S(2)}) async-start(f32[1,8,2,5,128]{4,2,3,0,1:T(2,128)} %copy.253), calls=%async_computation.2 | async-start | bytes 81920 | tf_op jit(solution)/shard_map/all_to_all | solution.py:164
  183.0 10.7 %copy-start.1 = (f32[8,32,128]{2,1,0:T(8,128)S(1)}, f32[8,32,128]{2,1,0:T(8,128)}, u32[]{:S(2)}) copy-start(f32[8,32,128]{2,1,0:T(8,128)} %param.9) | copy-start | bytes 393220
  193.1 2.3 %collective-permute-start.1 = (f32[5,1,32,128]{3,2,1,0:T(8,128)S(1)}, f32[5,1,32,128]{3,2,1,0:T(8,128)S(1)}, u32[]{:S(2)}, u32[]{:S(2)}) collective-permute-start(f32[5,1,32,128]{3,2,1,0:T(8,128)S(1)} %get-tuple-element.105), channel_id=1, source_target_pairs={{1,0},{2,1},{3,2},{0,3},{5,4},{6,5},{7,6},{4,7},{9,8},{10,9},{11,1... | collective-permute-start | bytes 245768 | tf_op jit(solution)/shard_map/ppermute | solution.py:22
  193.2 4.4 %collective-permute-start.2 = (f32[5,1,32,128]{3,2,1,0:T(8,128)S(1)}, f32[5,1,32,128]{3,2,1,0:T(8,128)S(1)}, u32[]{:S(2)}, u32[]{:S(2)}) collective-permute-start(f32[5,1,32,128]{3,2,1,0:T(8,128)S(1)} %get-tuple-element.106), channel_id=1, source_target_pairs={{0,1},{1,2},{2,3},{3,0},{4,5},{5,6},{6,7},{7,4},{8,9},{9,10},{10,1... | collective-permute-start | bytes 245768 | tf_op jit(solution)/shard_map/ppermute | solution.py:20
where the time goes:
time: 200 us; the launch traced here: 199 us
  local copies, waits for them, and re-layouts  137 us (68%)
  other arithmetic  33.4 us (17%)
  starting transfers between devices  17.6 us (9%)
  waiting for transfers between devices  10.5 us (5%)
    gather x16, local copies, waits for them, and re-layouts, gather_corners(): picks.append(data_flat[:, cells + shift_amount])  97.1 us
    scatter x1, other arithmetic, fill_fringe(): own = own.at[:, flat_nodes].set(jnp.where(live[None], interp, current))  29.7 us
    reshape x1, local copies, waits for them, and re-layouts, on_device(): filled = filled.reshape(width, planes, rows_count, cols_count)  10.1 us
    unnamed x6, local copies, waits for them, and re-layouts  9.78 us
    concatenate x1, local copies, waits for them, and re-layouts, on_device(): extended = jnp.concatenate([stacked, following], 1)  9.78 us
    scatter x1, local copies, waits for them, and re-layouts, fill_fringe(): jnp.zeros((own.shape[1],), own.dtype).at[flat_nodes]  8.1 us
    all_to_all x1, starting transfers between devices, on_device(): lax.all_to_all(donor_cell, 'grid', split_axis=1, concat_axis=1, tiled=True)  7.28 us
    all_to_all x1, waiting for transfers between devices, on_device(): lax.all_to_all(receptor_offset, 'grid', split_axis=1, concat_axis=1, tile...  6.52 us
  transfers between devices with their start and end apart: 6, of which 3 were waited for; matrix products, arithmetic and copies ran while one was open for 10% of the time, Pallas kernels for 0%

commit v1 on v0

v1 whole, which is shorter than its diff:
```python
import functools

import jax
import jax.numpy as jnp
from jax import lax
from jax.experimental import pallas as pl
from jax.experimental.pallas import tpu as pltpu
from jax.sharding import PartitionSpec as P

ROWS = 8
LANES = 128
UNROLL = 8
VMEM = pl.BlockSpec(memory_space=pltpu.VMEM)
SMEM = pl.BlockSpec(memory_space=pltpu.SMEM)
ANY = pl.BlockSpec(memory_space=pl.ANY)
LIMIT = 24 << 20


def passed_along(value, axis, steps):
    count = lax.axis_size(axis)
    pairs = [(source, (source + steps) % count) for source in range(count)]
    return lax.ppermute(value, axis, pairs)


def pack_kernel(count_ref, cell_ref, offset_ref, message_ref):
    owners, points = cell_ref.shape[1], cell_ref.shape[3]

    def one(owner, carry):
        cells = cell_ref[0, owner].astype(jnp.float32)
        count = count_ref[0, owner]
        counts = jnp.full((1, points), count, jnp.int32).astype(jnp.float32)
        message_ref[owner, 0:1, :] = cells[0:1]
        message_ref[owner, 1:4, :] = offset_ref[0, owner, 0]
        message_ref[owner, 4:5, :] = jnp.where(count > points, cells[1:2], counts)
        message_ref[owner, 5:8, :] = offset_ref[0, owner, 1]
        return carry

    lax.fori_loop(0, owners, one, 0, unroll=True)


def coefficients(corner):
    linear = [corner[4] - corner[0], corner[2] - corner[0], corner[1] - corner[0]]
    pair_01 = corner[6] - corner[4] - linear[1]
    pair_02 = corner[5] - corner[4] - linear[2]
    pair_12 = corner[3] - corner[2] - linear[2]
    triple = (corner[7] - corner[6]) - (corner[5] - corner[4]) - pair_12
    return corner[0], linear, pair_01, pair_02, pair_12, triple


def solve(corner, target):
    polys = []
    for component in range(3):
        start, linear, pair_01, pair_02, pair_12, triple = coefficients(
            [corner(q, component) for q in range(8)]
        )
        linear[component] = linear[component] + 1.0
        polys.append((start - target[component], linear, pair_01, pair_02, pair_12, triple))
    s0 = s1 = s2 = jnp.full(target[0].shape, 0.5, jnp.float32)
    for _ in range(4):
        s01, s02, s12 = s0 * s1, s0 * s2, s1 * s2
        misfit, jac = [], []
        for start, (l0, l1, l2), p01, p02, p12, triple in polys:
            d0 = l0 + s1 * p01 + s2 * p02 + s12 * triple
            d1 = l1 + s0 * p01 + s2 * p12 + s02 * triple
            d2 = l2 + s0 * p02 + s1 * p12 + s01 * triple
            misfit.append(start + s0 * d0 + s1 * (l1 + s2 * p12) + s2 * l2)
            jac.append((d0, d1, d2))
        (a0, a1, a2), (b0, b1, b2), (c0, c1, c2) = jac
        m0, m1, m2 = misfit
        bc12 = b1 * c2 - b2 * c1
        bc02 = b0 * c2 - b2 * c0
        bc01 = b0 * c1 - b1 * c0
        det = a0 * bc12 - a1 * bc02 + a2 * bc01
        bm2 = m1 * c2 - b2 * m2
        bm1 = m1 * c1 - b1 * m2
        bm0 = b0 * m2 - m1 * c0
        inverse = 1.0 / det
        u0 = m0 * bc12 - a1 * bm2 + a2 * bm1
        u1 = a0 * bm2 - m0 * bc02 + a2 * bm0
        u2 = a0 * (b1 * m2 - m1 * c1) - a1 * bm0 + m0 * bc01
        s0 = s0 - u0 * inverse
        s1 = s1 - u1 * inverse
        s2 = s2 - u2 * inverse
    values = []
    for variable in range(5):
        u = [corner(q, 3 + variable) for q in range(8)]
        e = [u[q] + s2 * (u[q + 1] - u[q]) for q in (0, 2, 4, 6)]
        f = [e[q] + s1 * (e[q + 1] - e[q]) for q in (0, 2)]
        values.append(f[0] + s0 * (f[1] - f[0]))
    return values


def gather_kernel(
    owners, field_ref, jitter_ref, next_ref, message_ref, message_any, out_ref,
    table, cells, picked, picked_more, sem,
):
    planes, rows_count = field_ref.shape[1], field_ref.shape[2]
    width = 8
    me = lax.axis_index("grid")
    heavy = lax.rem(me + owners - 1, owners)
    copies = [
        pltpu.make_async_copy(message_any.at[:, 4 * slot], cells.at[slot], sem.at[slot])
        for slot in range(2)
    ]
    for copy in copies:
        copy.start()

    blocks = rows_count // ROWS
    for variable in range(width):
        for plane in range(planes + 1):
            for block in range(blocks):
                place = pl.ds(block * ROWS, ROWS)
                if plane == planes:
                    tile = next_ref[variable, 0, place, :]
                elif variable < 3:
                    tile = jitter_ref[variable, plane, place, :]
                else:
                    tile = field_ref[variable - 3, plane, place, :]
                first = (plane * rows_count + block * ROWS) * width + variable
                table[pl.ds(first, ROWS, stride=width), :] = tile
    for copy in copies:
        copy.wait()

    lane = lax.broadcasted_iota(jnp.int32, (ROWS, LANES), 1)
    pair_of = lane >> 1
    even = (lane & 1) == 0
    steps = (0, 1, rows_count, rows_count + 1)

    def pick(slot, source, count):
        def chunk(step, held):
            held = list(held)
            for u in range(UNROLL):
                point = step * UNROLL + u
                cell = cells[slot, source, point].astype(jnp.int32)
                row, column = cell >> 7, cell & 127
                pair = step * (UNROLL // 2) + u // 2
                shift = (2 * pair - column) & 127
                mask = pair_of == pair
                for corner in range(4):
                    first = pl.multiple_of((row + steps[corner]) * width, width)
                    tile = pltpu.roll(table[pl.ds(first, width), :], shift, 1)
                    k = (u & 1) * 4 + corner
                    held[k] = jnp.where(mask, tile, held[k])
            return tuple(held)

        zero = jnp.zeros((width, LANES), jnp.float32)
        return lax.fori_loop(0, (count + UNROLL - 1) // UNROLL, chunk, (zero,) * 8)

    def one_source(source, carry):
        count = cells[1, source, 0].astype(jnp.int32)
        count = jnp.where(source == heavy, LANES, count)
        held = pick(0, source, count)
        for k in range(8):
            picked[pl.ds(k * width * owners + source, width, stride=owners), :] = held[k]
        return carry

    lax.fori_loop(0, owners, one_source, 0)
    held = pick(1, heavy, LANES)
    for k in range(8):
        picked_more[pl.ds(k * width, width), :] = held[k]

    def corner_of(read):
        def corner(q, variable):
            first = read(q >> 1, variable)
            second = read(4 + (q >> 1), variable)
            if q & 1:
                return jnp.where(even, pltpu.roll(first, LANES - 1, 1), second)
            return jnp.where(even, first, pltpu.roll(second, 1, 1))

        return corner

    def one_block(block, carry):
        def read(k, variable):
            first = (k * width + variable) * owners + block * ROWS
            return picked[pl.ds(pl.multiple_of(first, ROWS), ROWS), :]

        first = block * (ROWS * 8)
        target = [message_ref[pl.ds(first + 1 + c, ROWS, stride=8), :] for c in range(3)]
        values = solve(corner_of(read), target)
        for variable in range(5):
            place = pl.ds(block * (ROWS * 16) + variable, ROWS, stride=16)
            out_ref[place, :] = values[variable]
        return carry

    lax.fori_loop(0, owners // ROWS, one_block, 0, unroll=True)

    def read_more(k, variable):
        return jnp.broadcast_to(picked_more[pl.ds(k * width + variable, 1), :], (ROWS, LANES))

    target = [
        jnp.broadcast_to(message_ref[pl.ds(heavy * 8 + 5 + c, 1), :], (ROWS, LANES))
        for c in range(3)
    ]
    values = solve(corner_of(read_more), target)
    for variable in range(5):
        out_ref[pl.ds(heavy * 16 + 8 + variable, 1), :] = values[variable][0:1]


def relax_kernel(
    owners, node_ref, count_ref, field_ref, below_ref, above_ref, ratio_ref, values_ref, out_ref,
    table,
):
    variables, planes, rows_count, _ = field_ref.shape
    width = 8
    blocks = rows_count // ROWS
    plane_rows = rows_count * width

    def put(plane, block, variable, tile):
        first = plane * plane_rows + block * ROWS * width + variable
        table[pl.ds(first, ROWS, stride=width), :] = tile

    zero = jnp.zeros((ROWS, LANES), jnp.float32)
    for block in range(blocks):
        place = pl.ds(block * ROWS, ROWS)
        for variable in range(variables):
            put(0, block, variable, below_ref[variable, 0, place, :])
            put(planes + 1, block, variable, above_ref[3 + variable, 0, place, :])
            for plane in range(planes):
                put(plane + 1, block, variable, field_ref[variable, plane, place, :])
        for plane in range(planes):
            put(plane + 1, block, variables, zero)

    lane = lax.broadcasted_iota(jnp.int32, (ROWS, LANES), 1)
    sublane = lax.broadcasted_iota(jnp.int32, (ROWS, LANES), 0)

    def scatter(owner, slot, count):
        first = pl.multiple_of(owner * 16 + slot * 8, 8)
        tile = jnp.where(sublane == variables, 1.0, values_ref[pl.ds(first, 8), :])

        def one(point):
            node = node_ref[0, owner, slot, point]
            column = node & 127
            shift = (column - point) & 127
            first = pl.multiple_of(((node >> 7) + rows_count) * width, width)
            pltpu.store(
                table.at[pl.ds(first, width), :], pltpu.roll(tile, shift, 1), mask=lane == column
            )

        def chunk(step, carry):
            for u in range(UNROLL):
                one(step * UNROLL + u)
            return carry

        def single(point, carry):
            one(point)
            return carry

        full = count // UNROLL
        lax.fori_loop(0, full, chunk, 0)
        lax.fori_loop(full * UNROLL, count, single, 0)

    def one_owner(owner, carry):
        count = count_ref[0, owner]
        scatter(owner, 0, jnp.minimum(count, LANES))

        @pl.when(count > LANES)
        def _():
            scatter(owner, 1, count - LANES)

        return carry

    lax.fori_loop(0, owners, one_owner, 0)

    def one_plane(plane, carry):
        for block in range(blocks):
            ratio = ratio_ref[plane, pl.ds(block * ROWS, ROWS), :]
            inverse = 1.0 / (1.0 + 6.0 * ratio)
            base = pl.multiple_of((plane + 1) * plane_rows, plane_rows) + block * ROWS * width

            def get(step, variable):
                return table[pl.ds(base + step * width + variable, ROWS, stride=width), :]

            fringe = get(0, variables) > 0.5
            for variable in range(variables):
                here = get(0, variable)
                up, down = get(1, variable), get(-1, variable)
                if block == 0:
                    down = jnp.where(sublane == 0, 0.0, down)
                if block == blocks - 1:
                    up = jnp.where(sublane == ROWS - 1, 0.0, up)
                right = jnp.where(lane == LANES - 1, 0.0, pltpu.roll(here, LANES - 1, 1))
                left = jnp.where(lane == 0, 0.0, pltpu.roll(here, 1, 1))
                total = get(rows_count, variable) + get(-rows_count, variable)
                total = total + up + down + right + left
                smooth = (here + ratio * total) * inverse
                out_ref[variable, plane, pl.ds(block * ROWS, ROWS), :] = jnp.where(
                    fringe, here, smooth
                )
        return carry

    lax.fori_loop(0, planes, one_plane, 0)


def on_device(
    field, node_jitter, time_ratio, donor_cell, receptor_offset, receptor_node, point_count
):
    variables, planes, rows_count, cols_count = field.shape
    owners = donor_cell.shape[1]
    params = pltpu.CompilerParams(vmem_limit_bytes=LIMIT)
    first = jnp.concatenate([node_jitter[:, :1], field[:, :1]], 0)
    following = passed_along(first, "sub", -1)
    below = passed_along(field[:, planes - 1 :], "sub", 1)

    message = pl.pallas_call(
        pack_kernel,
        out_shape=jax.ShapeDtypeStruct((owners, 8, LANES), jnp.float32),
        in_specs=[SMEM, VMEM, VMEM],
        out_specs=VMEM,
        compiler_params=params,
        name="pack",
    )(point_count, donor_cell, receptor_offset)
    message = lax.all_to_all(message, "grid", split_axis=0, concat_axis=0, tiled=True)
    values = pl.pallas_call(
        functools.partial(gather_kernel, owners),
        out_shape=jax.ShapeDtypeStruct((owners * 16, LANES), jnp.float32),
        in_specs=[VMEM, VMEM, VMEM, VMEM, ANY],
        out_specs=VMEM,
        scratch_shapes=[
            pltpu.VMEM(((planes + 1) * rows_count * 8, LANES), jnp.float32),
            pltpu.SMEM((2, owners, LANES), jnp.float32),
            pltpu.VMEM((8 * 8 * owners, LANES), jnp.float32),
            pltpu.VMEM((8 * 8, LANES), jnp.float32),
            pltpu.SemaphoreType.DMA((2,)),
        ],
        compiler_params=params,
        name="gather",
    )(field, node_jitter, following, message.reshape(owners * 8, LANES), message)
    values = values.reshape(owners, 16, LANES)
    values = lax.all_to_all(values, "grid", split_axis=0, concat_axis=0, tiled=True)
    return pl.pallas_call(
        functools.partial(relax_kernel, owners),
        out_shape=jax.ShapeDtypeStruct(field.shape, jnp.float32),
        in_specs=[SMEM, SMEM, VMEM, VMEM, VMEM, VMEM, VMEM],
        out_specs=VMEM,
        scratch_shapes=[
            pltpu.VMEM(((planes + 2) * rows_count * 8, LANES), jnp.float32),
        ],
        compiler_params=params,
        name="relax",
    )(
        receptor_node, point_count, field, below, following, time_ratio,
        values.reshape(owners * 16, LANES),
    )


def solution(mesh):
    placed = (
        P(None, ("grid", "sub"), None, None),
        P(None, ("grid", "sub"), None, None),
        P(("grid", "sub"), None, None),
        P(("grid", "sub"), None, None, None),
        P(("grid", "sub"), None, None, None, None),
        P(("grid", "sub"), None, None, None),
        P(("grid", "sub"), None),
    )
    return jax.shard_map(
        on_device,
        mesh=mesh,
        in_specs=placed,
        out_specs=P(None, ("grid", "sub"), None, None),
        check_vma=False,
    )
```

time: 200 us -> 49.2 us (0.25)
  local copies, waits for them, and re-layouts: 137 us -> 2.84 us
  other arithmetic: 33.4 us -> 0.01 us
  Pallas kernels: 0 us -> 19.3 us
  blocking collectives: 0 us -> 12.3 us
  starting transfers between devices: 17.6 us -> 8.47 us
  waiting for transfers between devices: 10.5 us -> 6.9 us
    gather x16 -> x0, local copies, waits for them, and re-layouts: 97.1 us -> none  [gather_corners(): picks.append(data_flat[:, cells + shift_amount])]
    scatter x1 -> x0, other arithmetic: 29.7 us -> none  [fill_fringe(): own = own.at[:, flat_nodes].set(jnp.where(live[None], interp, current))]
    pallas_call x0 -> x3, Pallas kernels: none -> 19.3 us  [the longest x1 9.37 us: on_device(): pl.pallas_call(functools.partial(relax_kernel, owners), out_shape=jax.Sha...]
    all_to_all x0 -> x1, blocking collectives: none -> 12.3 us  [on_device(): lax.all_to_all(message, 'grid', split_axis=0, concat_axis=0, tiled=True)]
    concatenate x2 -> x0, local copies, waits for them, and re-layouts: 10.9 us -> none  [the longest x1 9.78 us: on_device(): extended = jnp.concatenate([stacked, following], 1)]
    all_to_all x3 -> x1, starting transfers between devices: 16.4 us -> 6.04 us  [on_device(): lax.all_to_all(values, 'grid', split_axis=0, concat_axis=0, tiled=True)]
    reshape x1 -> x0, local copies, waits for them, and re-layouts: 10.1 us -> none  [on_device(): filled = filled.reshape(width, planes, rows_count, cols_count)]
    unnamed x6 -> x15, local copies, waits for them, and re-layouts: 9.78 us -> 1.04 us
  transfers between devices with their start and end apart: 6 -> 3, of which waited for: 3 -> 2; matrix products, arithmetic and copies ran while one was open for 10% -> 0% of each run, Pallas kernels for 0% -> 1%
where the time goes in v1:
time: 49.2 us; the launch traced here: 49.9 us
  Pallas kernels  19.3 us (39%)
  blocking collectives  12.3 us (25%)
  starting transfers between devices  8.47 us (17%)
  waiting for transfers between devices  6.9 us (14%)
  local copies, waits for them, and re-layouts  2.84 us (6%)
    all_to_all x1, blocking collectives, on_device(): lax.all_to_all(message, 'grid', split_axis=0, concat_axis=0, tiled=True)  12.3 us
    pallas_call x1, Pallas kernels, on_device(): pl.pallas_call(functools.partial(relax_kernel, owners), out_shape=jax.Sha...  9.37 us
    pallas_call x1, Pallas kernels, on_device(): pl.pallas_call(functools.partial(gather_kernel, owners), out_shape=jax.Sh...  9.35 us
    all_to_all x1, starting transfers between devices, on_device(): lax.all_to_all(values, 'grid', split_axis=0, concat_axis=0, tiled=True)  6.04 us
    ppermute x2, waiting for transfers between devices, passed_along(): return lax.ppermute(value, axis, pairs)  3.86 us
    all_to_all x1, waiting for transfers between devices, on_device(): lax.all_to_all(values, 'grid', split_axis=0, concat_axis=0, tiled=True)  3.04 us
    ppermute x2, starting transfers between devices, passed_along(): return lax.ppermute(value, axis, pairs)  2.43 us
    slice x2, local copies, waits for them, and re-layouts, on_device(): first = jnp.concatenate([node_jitter[:, :1], field[:, :1]], 0)  1.81 us
  transfers between devices with their start and end apart: 3, of which 2 were waited for; matrix products, arithmetic and copies ran while one was open for 0% of the time, Pallas kernels for 1%

profile of v1, /device:TPU:0, one launch (start us, length us, event | category | flops | bytes accessed | tf_op | source)
XLA Modules:
  0.0 49.9 jit_solution(5476245767716741337)
XLA Ops:
  0.0 0.0 copy-start
  0.0 0.9 %slice.10 = f32[3,1,32,128]{3,2,1,0:T(8,128)S(1)} slice(f32[3,8,32,128]{3,2,1,0:T(8,128)} %jitter_ref.1), slice={[0:3], [0:1], [0:32], [0:128]} | slice | bytes 98304 | tf_op jit(solution)/shard_map/slice | solution.py:300
  0.9 0.9 %fusion = (f32[5,1,32,128]{3,2,1,0:T(8,128)S(1)}, f32[5,1,32,128]{3,2,1,0:T(8,128)S(1)}) fusion(f32[5,8,32,128]{3,2,1,0:T(8,128)} %field_ref.3), kind=kLoop, calls=%fused_computation.1 | loop fusion | bytes 327680 | tf_op jit(solution)/shard_map/slice | solution.py:300
  1.8 0.0 copy-start.6
  1.8 0.0 copy-start.4
  1.9 0.0 copy-start.5
  1.9 2.4 %collective-permute-start.1 = (f32[8,1,32,128]{3,2,1,0:T(8,128)S(1)}, f32[8,1,32,128]{3,2,1,0:T(8,128)S(1)}, u32[]{:S(2)}, u32[]{:S(2)}) collective-permute-start(f32[8,1,32,128]{3,2,1,0:T(8,128)S(1)} %pad_maximum_fusion), channel_id=1, source_target_pairs={{0,3},{1,0},{2,1},{3,2},{4,7},{5,4},{6,5},{7,6},{8,11},{9,8},{10,9... | collective-permute-start | bytes 393224 | tf_op jit(solution)/shard_map/ppermute | solution.py:22
  4.3 0.0 copy-done.6
  4.3 0.0 copy-done.4
  4.3 0.0 copy-done.5
  4.3 0.6 %pack.1 = f32[8,8,128]{2,1,0:T(8,128)S(1)} custom-call(s32[1,8]{1,0:T(1,128)S(1)} %copy-done.5, s32[1,8,2,128]{3,2,1,0:T(2,128)S(1)} %copy-done.4, f32[1,8,2,3,128]{4,3,2,1,0:T(4,128)S(1)} %copy.8.offset_ref), custom_call_target="tpu_custom_call" | custom-call | tf_op jit(solution)/shard_map/pack/pallas_call | solution.py:304
  4.9 12.3 %all_to_all.10.message_any = f32[8,8,128]{2,1,0:T(8,128)S(1)} all-to-all(f32[8,8,128]{2,1,0:T(8,128)S(1)} %pack.1), channel_id=1, replica_groups=mesh['grid'=8,'sub'=4] {'grid'}, dimensions={0} | all-to-all | bytes 65536 | tf_op jit(solution)/shard_map/all_to_all | solution.py:312
  17.2 0.0 collective-permute-done.1.next_ref.above_ref
  17.2 0.0 copy-done
  17.2 0.0 copy-start.1
  17.2 1.0 %copy-done.1 = f32[3,8,32,128]{3,2,1,0:T(8,128)S(1)} copy-done((f32[3,8,32,128]{3,2,1,0:T(8,128)S(1)}, f32[3,8,32,128]{3,2,1,0:T(8,128)}, u32[]{:S(2)}) %copy-start.1) | copy-done | bytes 393240
  18.2 0.0 copy-start.3
  18.2 9.4 %gather.1 = f32[128,128]{1,0:T(8,128)} custom-call(f32[5,8,32,128]{3,2,1,0:T(8,128)S(1)} %copy-done, f32[3,8,32,128]{3,2,1,0:T(8,128)S(1)} %copy-done.1, f32[8,1,32,128]{3,2,1,0:T(8,128)S(1)} %collective-permute-done.1.next_ref.above_ref, f32[64,128]{1,0:T(8,128)S(1)} %bitcast.3, f32[8,8,128]{2,1,0:T(8,128)S(1)} %all_to_all.10.message_any), custom_call_target="tpu_custom_call" | custom-call | tf_op jit(solution)/shard_map/gather/pallas_call | solution.py:313
  27.6 0.0 copy-start.2
  27.6 6.0 %all-to-all-start.1 = ((f32[8,16,128]{2,1,0:T(8,128)}), f32[8,16,128]{2,1,0:T(8,128)S(1)}, u32[]{:S(2)}, u32[]{:S(2)}) async-start(f32[8,16,128]{2,1,0:T(8,128)} %bitcast.1), calls=%async_computation.1 | async-start | bytes 131072 | tf_op jit(solution)/shard_map/all_to_all | solution.py:329
  33.6 0.0 collective-permute-start
  33.6 3.9 %collective-permute-done.below_ref = f32[5,1,32,128]{3,2,1,0:T(8,128)S(1)} collective-permute-done((f32[5,1,32,128]{3,2,1,0:T(8,128)S(1)}, f32[5,1,32,128]{3,2,1,0:T(8,128)S(1)}, u32[]{:S(2)}, u32[]{:S(2)}) %collective-permute-start) | collective-permute-done | bytes 81952 | tf_op jit(solution)/shard_map/ppermute | solution.py:22
  37.5 3.0 %all-to-all-done.1 = f32[8,16,128]{2,1,0:T(8,128)S(1)} async-done(((f32[8,16,128]{2,1,0:T(8,128)}), f32[8,16,128]{2,1,0:T(8,128)S(1)}, u32[]{:S(2)}, u32[]{:S(2)}) %all-to-all-start.1) | async-done | bytes 65568 | tf_op jit(solution)/shard_map/all_to_all | solution.py:329
  40.5 0.0 copy-done.3
  40.5 0.0 copy-done.2
  40.5 9.4 %relax.1 = f32[5,8,32,128]{3,2,1,0:T(8,128)} custom-call(s32[1,8,2,128]{3,2,1,0:T(2,128)S(1)} %copy-done.3, s32[1,8]{1,0:T(1,128)S(1)} %copy-done.5, f32[5,8,32,128]{3,2,1,0:T(8,128)S(1)} %copy-done, f32[5,1,32,128]{3,2,1,0:T(8,128)S(1)} %collective-permute-done.below_ref, f32[8,1,32,128]{3,2,1,0:T(8,128)S(1)} %collective-permute-done.1.next_ref.above_ref, ...), custom_call_target="tpu_custom_call" | custom-call | tf_op jit(solution)/shard_map/relax/pallas_call | solution.py:330
  (2 shorter events, 0.0 us)
Async XLA Ops:
  0.0 17.2 %copy-start = (f32[5,8,32,128]{3,2,1,0:T(8,128)S(1)}, f32[5,8,32,128]{3,2,1,0:T(8,128)}, u32[]{:S(2)}) copy-start(f32[5,8,32,128]{3,2,1,0:T(8,128)} %field_ref.3) | copy-start | bytes 1966084
  1.8 2.5 %copy-start.6 = (f32[1,8,2,3,128]{4,2,3,1,0:T(2,128)S(1)}, f32[1,8,2,3,128]{4,2,3,1,0:T(2,128)}, u32[]{:S(2)}) copy-start(f32[1,8,2,3,128]{4,2,3,1,0:T(2,128)} %param.11) | copy-start | bytes 73732
  1.8 2.5 %copy-start.4 = (s32[1,8,2,128]{3,2,1,0:T(2,128)S(1)}, s32[1,8,2,128]{3,2,1,0:T(2,128)}, u32[]{:S(2)}) copy-start(s32[1,8,2,128]{3,2,1,0:T(2,128)} %cell_ref.1) | copy-start | bytes 24580
  1.9 2.5 %copy-start.5 = (s32[1,8]{1,0:T(1,128)S(1)}, s32[1,8]{1,0:T(1,128)}, u32[]{:S(2)}) copy-start(s32[1,8]{1,0:T(1,128)} %count_ref.3) | copy-start | bytes 100
  1.9 15.4 %collective-permute-start.1 = (f32[8,1,32,128]{3,2,1,0:T(8,128)S(1)}, f32[8,1,32,128]{3,2,1,0:T(8,128)S(1)}, u32[]{:S(2)}, u32[]{:S(2)}) collective-permute-start(f32[8,1,32,128]{3,2,1,0:T(8,128)S(1)} %pad_maximum_fusion), channel_id=1, source_target_pairs={{0,3},{1,0},{2,1},{3,2},{4,7},{5,4},{6,5},{7,6},{8,11},{9,8},{10,9... | collective-permute-start | bytes 393224 | tf_op jit(solution)/shard_map/ppermute | solution.py:22
  17.2 1.0 %copy-start.1 = (f32[3,8,32,128]{3,2,1,0:T(8,128)S(1)}, f32[3,8,32,128]{3,2,1,0:T(8,128)}, u32[]{:S(2)}) copy-start(f32[3,8,32,128]{3,2,1,0:T(8,128)} %jitter_ref.1) | copy-start | bytes 1179652
  18.2 22.3 %copy-start.3 = (s32[1,8,2,128]{3,2,1,0:T(2,128)S(1)}, s32[1,8,2,128]{3,2,1,0:T(2,128)}, u32[]{:S(2)}) copy-start(s32[1,8,2,128]{3,2,1,0:T(2,128)} %node_ref.1) | copy-start | bytes 24580
  27.6 13.0 %copy-start.2 = (f32[8,32,128]{2,1,0:T(8,128)S(1)}, f32[8,32,128]{2,1,0:T(8,128)}, u32[]{:S(2)}) copy-start(f32[8,32,128]{2,1,0:T(8,128)} %ratio_ref.1) | copy-start | bytes 393220
  27.6 12.9 %all-to-all-start.1 = ((f32[8,16,128]{2,1,0:T(8,128)}), f32[8,16,128]{2,1,0:T(8,128)S(1)}, u32[]{:S(2)}, u32[]{:S(2)}) async-start(f32[8,16,128]{2,1,0:T(8,128)} %bitcast.1), calls=%async_computation.1 | async-start | bytes 131072 | tf_op jit(solution)/shard_map/all_to_all | solution.py:329
  33.6 3.9 %collective-permute-start = (f32[5,1,32,128]{3,2,1,0:T(8,128)S(1)}, f32[5,1,32,128]{3,2,1,0:T(8,128)S(1)}, u32[]{:S(2)}, u32[]{:S(2)}) collective-permute-start(f32[5,1,32,128]{3,2,1,0:T(8,128)S(1)} %get-tuple-element.6), channel_id=1, source_target_pairs={{0,1},{1,2},{2,3},{3,0},{4,5},{5,6},{6,7},{7,4},{8,9},{9,10},{10,1... | collective-permute-start | bytes 245768 | tf_op jit(solution)/shard_map/ppermute | solution.py:22
